TPU v7x, 32 devices: a whole 2x2x4 slice. The times are simulated.
32 devices in a mesh: lat: 4 (over y, x), fld: 8 (over z, core).
Axes of the slice: x: 2, y: 2, z: 4, core: 2. Of those that a mesh axis runs over, the one named last changes fastest.
Arguments:
- patches: bfloat16 [64, 16, 32, 512], P('fld', 'lat'), may hold values from -6 to 6
- segment_ids: int32 [64, 16, 32], P('fld'), may hold values from 0 to 2, as said below
- gain_attn: float32 [512], replicated, may hold values from 0.25 to 1.75
- bias_attn: float32 [512], replicated, may hold values from -2 to 2
- w_qkv: bfloat16 [512, 1536], replicated, may hold values from -0.25 to 0.25
- w_proj: bfloat16 [512, 512], replicated, may hold values from -0.5 to 0.5
- gain_mlp: float32 [512], replicated, may hold values from 0.25 to 1.75
- bias_mlp: float32 [512], replicated, may hold values from -2 to 2
- w_hidden: bfloat16 [512, 2048], replicated, may hold values from -0.25 to 0.25
- w_output: bfloat16 [2048, 512], replicated, may hold values from -0.1875 to 0.1875
- cotangent: bfloat16 [64, 16, 32, 512], P('fld', 'lat'), may hold values from -6 to 6
Outputs:
- layer_out: bfloat16 [64, 16, 32, 512], P('fld', 'lat')
- patch_grad: float32 [64, 16, 32, 512], P('fld', 'lat')
- attn_gain_grad: float32 [512], replicated
- attn_bias_grad: float32 [512], replicated
- qkv_grad: float32 [512, 1536], replicated
- proj_grad: float32 [512, 512], replicated
- mlp_gain_grad: float32 [512], replicated
- mlp_bias_grad: float32 [512], replicated
- hidden_grad: float32 [512, 2048], replicated
- output_grad: float32 [2048, 512], replicated
Inputs may be any that keep to these rules, and one draw needn't show every extreme that they name: `segment_ids`: within a field the ids are the same in all 16 rows of a column and never fall from column 0 to column 31; column 0 holds 0 and the last column 2.
All inputs are finite; a program needn't handle non-finite values.
Results may differ from a plain program's by a relative error of at most 0.01.
Values may be sent and summed in bfloat16 or wider, within the bound.
A program may use at most 448 MiB of HBM per device.

v0:
```python
import functools
import math

import jax
import jax.numpy as jnp
from jax import lax
from jax.experimental import pallas as pl
from jax.experimental.pallas import tpu as pltpu
from jax.sharding import PartitionSpec as P

HEAD_DIM = 32
GROUP = 8
WIDE = GROUP * HEAD_DIM
SCALE = HEAD_DIM ** -0.5
LOG2E = math.log2(math.e)
EPS = 1e-6
REACH = 4
NEG = -1e30
CHUNK = 512
BLOCK = 256
FIELDS_AT_ONCE = 2
DIRECT = (5, 6)
Z_FIRST = ()
SCHEDULE = {
    "J2": (0, 1),
    "J4": (0, 2, 3, 1),
    "J6": (2, 3, 4, 5),
    "J8": (4, 6, 7, 5),
    "E0": (0, 1),
    "E1": (6, 7),
    "E2": (2, 3),
    "P1": (4, 5, 8, 9),
    "A1": (8,),
    "A2": (9, 0),
    "A3": (1,),
    "B1": (7,),
    "B2": (0, 6),
    "B3": (2, 1),
    "D0": (4,),
    "D1": (3, 9),
    "D2": (0,),
    "D3": (6,),
    "X": (2,),
    "X1": (1, 5, 4, 0, 8),
    "X2": (3, 7),
    "C0": (9, 6, 10),
    "X3": (8, 1, 2),
    "X4": (10, 5),
    "C1": (0, 4, 12),
    "F1": (3, 0),
    "F2": (1, 7, 12),
    "F3": (9, 2),
    "V0": (14,),
    "T": (6, 1, 8, 3, 5, 10, 14, 7, 9, 4, 8, 12, 10, 14, 2, 6, 5, 7, 9, 3, 12, 14, 2, 8, 3, 4, 10, 5, 6, 4, 12, 5, 8, 7, 6, 9, 8, 7, 9, 10, 10, 12, 12),
}
BF = jnp.bfloat16
F32 = jnp.float32
MESH = pl.DeviceIdType.MESH

NT = (((1,), (1,)), ((), ()))
TN = (((0,), (0,)), ((), ()))


def dot(a, b, dims=None):
    if dims is None:
        return jnp.dot(a, b, preferred_element_type=F32)
    return lax.dot_general(a, b, dims, preferred_element_type=F32)


def normalize(x):
    center = jnp.mean(x, axis=-1, keepdims=True)
    off = x - center
    rstd = lax.rsqrt(jnp.mean(off * off, axis=-1, keepdims=True) + EPS)
    return off * rstd, rstd


def norm_pull(e, gain, n, rstd):
    ge = e * gain
    a = jnp.mean(ge, axis=-1, keepdims=True)
    b = jnp.mean(ge * n, axis=-1, keepdims=True)
    return (ge - a - n * b) * rstd


def gelu_both(u):
    cdf = 0.5 + 0.5 * lax.erf(u * (1.0 / math.sqrt(2.0)))
    density = jnp.exp2((u * u) * (-0.5 * LOG2E)) * (1.0 / math.sqrt(2.0 * math.pi))
    return u * cdf, cdf + u * density


def row_sums(x):
    return jnp.sum(x, axis=0, keepdims=True)


class Plan:
    def __init__(self, mesh, fields, rows, cols, width, ff):
        self.lats = mesh.shape["lat"]
        self.flds = mesh.shape["fld"]
        self.zs = self.flds // 2
        self.fields, self.rows, self.cols = fields, rows, cols
        self.tf = rows * cols
        self.tokens = fields * self.tf
        self.width, self.ff = width, ff
        self.chunks = ff // CHUNK
        self.size_of = {"core": 2, "x": 2, "y": self.lats // 2, "lat": self.lats, "z": self.zs}
        unit = 16 * self.lats * self.flds
        blocks = width // 128
        mlp = CHUNK * blocks + width * (CHUNK // 128)
        rows_needed = [mlp] * self.chunks + [width * blocks] + [width * (3 * WIDE // 128)] * 2
        self.sizes, self.subs = [], []
        for p, n in enumerate(rows_needed):
            n = -(-n // unit) * unit
            self.sizes.append(n)
            if p in Z_FIRST:
                self.subs.append([(0, n, ("core", "z", "lat"))])
            elif p in DIRECT or n % (2 * unit):
                self.subs.append([(0, n, ("core", "lat", "z"))])
            else:
                self.subs.append([(0, n // 2, ("core", "x", "y", "z")), (n // 2, n // 2, ("core", "y", "x", "z"))])
        self.landing = []
        for subs in self.subs:
            total = 0
            for _, n, order in subs:
                for d in order:
                    n //= self.size_of[d]
                    total += n * (self.size_of[d] - 1)
            self.landing.append(total)
        self.n_subs = sum(len(s) for s in self.subs)


def body(plan, *refs):
    pn = plan
    np_ = len(pn.sizes)
    (patches, seg, gain_a, bias_a, w_qkv, w_proj, gain_m, bias_m, w_hid, w_out, cot) = refs[:11]
    out_layer, out_patch, out_vec = refs[11:14]
    out_ag = refs[14 : 14 + np_]
    sc = list(refs[14 + np_ :])

    def take(n):
        got = sc[:n]
        del sc[:n]
        return got

    wq, wp, wh, wo = take(4)
    pb, cb, segv, halo = take(4)
    normed, qb, kv, pt, ctx, res, nm, gres, act, gpre, gctx, edge = take(12)
    hq, hg, lse, hlse, dst, hdst = take(6)
    bm, biasb, vec, vrz, vrx, vrc = take(6)
    sb, rb, ag = take(np_), take(np_), take(np_)
    in_sem, out_sem, halo_s, halo_r, rim_s, rim_r, back_s, back_r, rs_s, rs_r, v_s, v_r = take(12)

    lat = lax.axis_index("lat")
    fld = lax.axis_index("fld")
    core = lax.rem(fld, 2)
    z = lax.div(fld, 2)
    x = lax.rem(lat, 2)
    y = lax.div(lat, 2)
    L, Z, Y = pn.lats, pn.zs, pn.lats // 2
    FD, R, C, TF, T, D, FF = pn.fields, pn.rows, pn.cols, pn.tf, pn.tokens, pn.width, pn.ff

    ins = [(patches, pb), (w_qkv, wq), (seg, segv), (cot, cb), (w_out, wo), (w_proj, wp), (w_hid, wh)]
    loads = [pltpu.make_async_copy(s, d, in_sem.at[i]) for i, (s, d) in enumerate(ins)]
    loads[0].start()
    loads[1].start()

    me = {"core": core, "x": x, "y": y, "lat": lat, "z": z}

    def device(d, i):
        if d == "core":
            return lat, z * 2 + i
        if d == "x":
            return y * 2 + i, fld
        if d == "y":
            return i * 2 + x, fld
        if d == "lat":
            return i, fld
        return lat, i * 2 + core

    def peers(d):
        n = pn.size_of[d]
        places = [lax.rem(me[d] + k, n) for k in range(1, n)]
        return [(i, device(d, i)) for i in places]

    barrier = pltpu.get_barrier_semaphore()
    everyone = peers("core") + peers("lat") + peers("z")
    for _, dev in everyone:
        pl.semaphore_signal(barrier, inc=1, device_id=dev, device_id_type=MESH)
    pl.semaphore_wait(barrier, len(everyone))

    up, down = (lat - 1, fld), (lat + 1, fld)
    has_up, has_down = lat > 0, lat < L - 1

    def remote(src, dst, s, r, dev):
        return pltpu.make_async_remote_copy(
            src_ref=src, dst_ref=dst, send_sem=s, recv_sem=r, device_id=dev, device_id_type=MESH
        )

    def arrived(ref, sem):
        pltpu.make_async_copy(ref, ref, sem).wait()

    half = FD // 2
    halo_copies = []
    for h in range(2):
        some = pl.ds(h * half, half)
        to_up = remote(patches.at[some, pl.ds(0, C)], halo.at[1, some], halo_s.at[0, h], halo_r.at[1, h], up)
        to_dn = remote(patches.at[some, pl.ds(TF - C, C)], halo.at[0, some], halo_s.at[1, h], halo_r.at[0, h], down)
        pl.when(has_up)(to_up.start)
        pl.when(has_down)(to_dn.start)
        halo_copies.append((to_up, to_dn))
    for c in loads[2:]:
        c.start()

    def spot(off, n):
        return pl.ds(pl.multiple_of(off, 16), n)

    class Part:
        def __init__(self, p, number, start, n, order, land):
            self.p, self.number, self.order = p, number, order
            self.off, self.len, self.land = [start], [n], []
            for d in order:
                g = pn.size_of[d]
                n = n // g
                self.land.append(land)
                land += n * (g - 1)
                self.off.append(self.off[-1] + me[d] * n)
                self.len.append(n)
            self.end = land

        def moved(self, i):
            return self.len[i + 1] * (pn.size_of[self.order[i]] - 1)

        def scatter(self, i):
            n = self.len[i + 1]
            for k, (j, dev) in enumerate(peers(self.order[i])):
                src = sb[self.p].at[spot(self.off[i] + j * n, n)]
                dst = rb[self.p].at[pl.ds(self.land[i] + k * n, n)]
                remote(src, dst, rs_s.at[self.number, i], rs_r.at[self.number, i], dev).start()

        def add(self, i):
            n = self.len[i + 1]
            d = self.order[i]
            arrived(rb[self.p].at[pl.ds(self.land[i], self.moved(i))], rs_r.at[self.number, i])
            mine = spot(self.off[i + 1], n)
            total = sb[self.p][mine, :].astype(F32)
            for k in range(pn.size_of[d] - 1):
                total = total + rb[self.p][self.land[i] + k * n : self.land[i] + (k + 1) * n, :].astype(F32)
            to = ag if i == len(self.order) - 1 else sb
            to[self.p][mine, :] = total.astype(BF)

        def gather(self, i):
            s = 4 + i
            mine = ag[self.p].at[spot(self.off[i + 1], self.len[i + 1])]
            for _, dev in peers(self.order[i]):
                remote(mine, mine, rs_s.at[self.number, s], rs_r.at[self.number, s], dev).start()

        def gathered(self, i):
            arrived(ag[self.p].at[pl.ds(0, self.moved(i))], rs_r.at[self.number, 4 + i])

        def step(self, s):
            nd = len(self.order)
            if s < nd:
                if s > 0:
                    self.add(s - 1)
                self.scatter(s)
            elif s == nd:
                self.add(nd - 1)
                self.gather(nd - 1)
            else:
                self.gathered(2 * nd - s)
                if s < 2 * nd:
                    self.gather(2 * nd - 1 - s)

        def finish(self):
            for i in range(len(self.order)):
                for s in (i, 4 + i):
                    arrived(sb[self.p].at[pl.ds(0, self.moved(i))], rs_s.at[self.number, s])

    parts, number = [], 0
    for p in range(np_):
        mine, land = [], 0
        for start, n, order in pn.subs[p]:
            mine.append(Part(p, number, start, n, order, land))
            land = mine[-1].end
            number += 1
        parts.append(mine)
    every = [part for mine in parts for part in mine]
    vec_at = len(every)
    reached = [0] * (vec_at + 1)
    last_step = [2 * len(part.order) for part in every] + [3]

    def out_copy(part):
        rows = pl.ds(part.off[0], part.len[0])
        return pltpu.make_async_copy(ag[part.p].at[rows], out_ag[part.p].at[rows], out_sem.at[2 + part.number])

    codes = [2 * p + i for p, mine in enumerate(parts) for i in range(len(mine))] + [2 * np_]
    number_of = {code: k for k, code in enumerate(codes)}

    def hook(*some):
        steps = []
        for code in some:
            k = number_of.get(code, vec_at + 1)
            if k <= vec_at and reached[k] <= last_step[k]:
                steps.append((k, reached[k]))
                reached[k] += 1

        def run():
            for k, s in steps:
                if k == vec_at:
                    vec_step(s)
                    continue
                every[k].step(s)
                if s == last_step[k]:
                    out_copy(every[k]).start()

        return run

    def place(name):
        return hook(*SCHEDULE.get(name, ()))

    rounds = ((vrz, "z"), (vrx, "lat"), (vrc, "core"))

    def vec_step(s):
        if s > 0:
            buf, d = rounds[s - 1]
            count = pn.size_of[d]
            arrived(buf.at[pl.ds(0, count - 1)], v_r.at[s - 1])
            arrived(buf.at[pl.ds(0, count - 1)], v_s.at[s - 1])
            total = buf[0]
            for k in range(1, count):
                total = total + buf[k]
            vec[...] = total
        if s < 3:
            buf, d = rounds[s]
            buf[me[d]] = vec[...]
            for _, dev in peers(d):
                remote(vec, buf.at[me[d]], v_s.at[s], v_r.at[s], dev).start()
        else:
            pltpu.make_async_copy(vec, out_vec, in_sem.at[0]).start()

    def finish(part):
        part.finish()
        out_copy(part).wait()

    def put(p, start, stride, value):
        rows, lanes = value.shape
        low = value.astype(BF)
        for j in range(lanes // 128):
            at = start + j * stride
            sb[p][at : at + rows, :] = low[:, j * 128 : (j + 1) * 128]

    rid = lax.broadcasted_iota(jnp.int32, (WIDE, WIDE), 0) // HEAD_DIM
    cid = lax.broadcasted_iota(jnp.int32, (WIDE, WIDE), 1) // HEAD_DIM
    same = jnp.where(rid == cid, 1.0, 0.0)
    bm[...] = same.astype(BF)

    ga, ba = gain_a[...].reshape(1, D), bias_a[...].reshape(1, D)
    gm, bmlp = gain_m[...].reshape(1, D), bias_m[...].reshape(1, D)
    loads[0].wait()

    per = max(1, 256 // TF)
    tile = per * TF
    tiles = T // tile

    def rows_at(t):
        return slice(t * tile, (t + 1) * tile)

    def fields_at(t):
        return slice(t * per, (t + 1) * per)

    def norm_one(t):
        n, _ = normalize(pb[fields_at(t)].reshape(tile, D).astype(F32))
        normed[rows_at(t), :] = (n * ga + ba).astype(BF)

    norm_one(0)
    loads[1].wait()
    for t in range(tiles):
        if t + 1 < tiles:
            norm_one(t + 1)
        qb[rows_at(t), :] = dot(normed[rows_at(t), :], wq[:, :D]).astype(BF)
        part = dot(normed[rows_at(t), :], wq[:, D:]).astype(BF)
        kv[fields_at(t), C : C + TF, :] = part.reshape(per, TF, 2 * D)

    loads[2].wait()
    kcol = lax.broadcasted_iota(jnp.int32, (C, WIDE), 0)
    qcol = lax.rem(lax.broadcasted_iota(jnp.int32, (C, WIDE), 1), C)
    away = jnp.abs(kcol - qcol)
    near = jnp.minimum(away, C - away) <= REACH
    diag = lax.broadcasted_iota(jnp.int32, (C, C), 0) == lax.broadcasted_iota(jnp.int32, (C, C), 1)
    for f in range(FD):
        line = segv[f, 0:1, :].astype(F32)
        across = jnp.concatenate([line] * GROUP, axis=1)
        along = jnp.sum(jnp.where(diag, line, 0.0), axis=1, keepdims=True)
        biasb[f] = jnp.where(jnp.logical_and(near, along == across), 0.0, NEG)
    pole_top = jnp.where(has_up, 0.0, NEG)
    pole_bottom = jnp.where(has_down, 0.0, NEG)

    lane_head = lax.broadcasted_iota(jnp.int32, (HEAD_DIM, WIDE), 1) // HEAD_DIM

    def diagonal(o):
        total = o[0:HEAD_DIM]
        for h in range(1, GROUP):
            total = jnp.where(lane_head == h, o[h * HEAD_DIM : (h + 1) * HEAD_DIM], total)
        return total

    def widened(q):
        return jnp.concatenate([q] * GROUP, axis=0) * bm[...]

    fpi = min(FIELDS_AT_ONCE, FD)

    def span(f, row):
        return pl.ds(pl.multiple_of(f * TF + row * C, C), C)

    k_lanes = [slice(g * WIDE, (g + 1) * WIDE) for g in range(2)]
    v_lanes = [slice(D + g * WIDE, D + (g + 1) * WIDE) for g in range(2)]

    def attend(rows, i, carry):
        units = [(i * fpi + j, g, r) for j in range(fpi) for g in range(2) for r in rows]
        scores = []
        for f, g, r in units:
            k = kv[f, r * C : (r + 3) * C, k_lanes[g]]
            scores.append(dot(k, widened(qb[span(f, r), k_lanes[g]]), NT))
        low, logs = [], []
        for (f, g, r), s in zip(units, scores):
            bias = biasb[f]
            first = bias + pole_top if r == 0 else bias
            third = bias + pole_bottom if r == R - 1 else bias
            s = s + jnp.concatenate([first, bias, third], axis=0)
            m = jnp.max(s, axis=0, keepdims=True)
            p = jnp.exp2((s - m) * (SCALE * LOG2E))
            total = row_sums(p)
            logs.append(m * (SCALE * LOG2E) + jnp.log2(total) if r in (0, R - 1) else None)
            low.append((p * (1.0 / total)).astype(BF))
        outs = []
        for (f, g, r), p in zip(units, low):
            v = kv[f, r * C : (r + 3) * C, v_lanes[g]]
            outs.append(diagonal(dot(p, v, TN)).astype(BF))
        for (f, g, r), p, log, o in zip(units, low, logs, outs):
            pt[f, g * R + r] = p
            ctx[span(f, r), k_lanes[g]] = o
            if r in (0, R - 1):
                lse[0 if r == 0 else 1, pl.ds(f * 2 + g, 1), :] = log
        return carry

    if R > 2:
        lax.fori_loop(0, FD // fpi, functools.partial(attend, range(1, R - 1)), 0)

    loads[3].wait()
    loads[4].wait()
    for j in range(FF // BLOCK):
        some = slice(j * BLOCK, (j + 1) * BLOCK)
        gpre[:, some] = dot(cb[...], wo[some, :], NT).astype(BF)

    for h in range(2):
        some = slice(h * half, (h + 1) * half)
        flat = slice(h * half * C, (h + 1) * half * C)
        for side, ok, copy in ((0, has_up, halo_copies[h][1]), (1, has_down, halo_copies[h][0])):
            pl.when(ok)(copy.wait_recv)

            @pl.when(jnp.logical_not(ok))
            def _():
                halo[side, some] = jnp.zeros((half, C, D), BF)

            n, _unused = normalize(halo[side, some].reshape(half * C, D).astype(F32))
            low = (n * ga + ba).astype(BF)
            hq[side, flat, :] = dot(low, wq[:, :D]).astype(BF)
            start = 0 if side == 0 else TF + C
            kv[some, start : start + C, :] = dot(low, wq[:, D:]).astype(BF).reshape(half, C, 2 * D)
        turns = half // fpi
        lax.fori_loop(h * turns, (h + 1) * turns, functools.partial(attend, (0, R - 1)), 0)

    loads[5].wait()
    for t in range(tiles):
        r = pb[fields_at(t)].reshape(tile, D).astype(F32) + dot(ctx[rows_at(t), :], wp[...])
        res[rows_at(t), :] = r
        n, _ = normalize(r)
        nm[rows_at(t), :] = (n * gm + bmlp).astype(BF)

    loads[6].wait()
    blocks = FF // BLOCK
    in_chunk = CHUNK // BLOCK

    def hidden_block(j):
        return slice(j * BLOCK, (j + 1) * BLOCK)

    def kept(ref, j):
        return ref.at[pl.ds(0, T), pl.ds((j % 2) * BLOCK, BLOCK)]

    def mlp_in(j):
        kept(gres, j)[...] = dot(nm[...], wh[:, hidden_block(j)])

    def mlp_mid(j):
        a, da = gelu_both(kept(gres, j)[...])
        act[:, hidden_block(j)] = a.astype(BF)
        gpre[:, hidden_block(j)] = (da * gpre[:, hidden_block(j)].astype(F32)).astype(BF)

    def mlp_out(j):
        c, part = j // in_chunk, j % in_chunk
        put(c, part * BLOCK, CHUNK, dot(act[:, hidden_block(j)], cb[...], TN))
        start = CHUNK * (D // 128) + part * (BLOCK // 128) * D
        put(c, start, D, dot(nm[...], gpre[:, hidden_block(j)], TN))

    mlp_in(0)
    for j in range(blocks):
        if j + 1 < blocks:
            mlp_in(j + 1)
        mlp_mid(j)
        if j > 0:
            mlp_out(j - 1)
        place(f"J{j}")()
    mlp_out(blocks - 1)
    place(f"J{blocks}")()

    zero = jnp.zeros((1, D), F32)

    mlp_gain, mlp_bias = zero, zero

    l_up = remote(lse.at[0], hlse.at[1], back_s.at[2], back_r.at[3], up)
    l_dn = remote(lse.at[1], hlse.at[0], back_s.at[3], back_r.at[2], down)
    pl.when(has_up)(l_up.start)
    pl.when(has_down)(l_dn.start)

    head_rows = lax.broadcasted_iota(jnp.int32, (2 * GROUP, D), 0) == lax.broadcasted_iota(
        jnp.int32, (2 * GROUP, D), 1
    ) // HEAD_DIM
    head_rows = jnp.where(head_rows, 1.0, 0.0).astype(BF)
    own_head = lax.broadcasted_iota(jnp.int32, (GROUP, WIDE), 0) == lax.broadcasted_iota(
        jnp.int32, (GROUP, WIDE), 1
    ) // HEAD_DIM

    def rim_totals(some):
        spots = [(f, side) for f in range(some.start, some.stop) for side in range(2)]
        terms = []
        for f, side in spots:
            row = 0 if side == 0 else R - 1
            mine = ctx[f * TF + row * C : f * TF + (row + 1) * C, :].astype(F32)
            terms.append(mine * gctx[f, row * C : (row + 1) * C, :].astype(F32))
        terms = jnp.concatenate(terms, axis=0)
        high = terms.astype(BF)
        rest = (terms - high.astype(F32)).astype(BF)
        sums = dot(head_rows, high, NT) + dot(head_rows, rest, NT)
        for i, (f, side) in enumerate(spots):
            across = jnp.concatenate([sums[:, i * C : (i + 1) * C]] * GROUP, axis=1)
            for g in range(2):
                own = jnp.where(own_head, across[g * GROUP : (g + 1) * GROUP], 0.0)
                dst[side, 2 * f + g : 2 * f + g + 1, :] = row_sums(own)

    def send_rims(some):
        some = pl.ds(some.start, some.stop - some.start)
        h = some.start // half
        to_up = remote(gctx.at[some, pl.ds(0, C)], hg.at[1, some], rim_s.at[0, h], rim_r.at[1, h], up)
        to_dn = remote(gctx.at[some, pl.ds(TF - C, C)], hg.at[0, some], rim_s.at[1, h], rim_r.at[0, h], down)
        pl.when(has_up)(to_up.start)
        pl.when(has_down)(to_dn.start)

    grad_in = dot(gpre[rows_at(0), :], wh[...], NT)
    for t in range(tiles):
        e = grad_in
        if t + 1 < tiles:
            grad_in = dot(gpre[rows_at(t + 1), :], wh[...], NT)
        n, rstd = normalize(res[rows_at(t), :])
        gr = cb[rows_at(t), :].astype(F32) + norm_pull(e, gm, n, rstd)
        gres[rows_at(t), :] = gr
        low = gr.astype(BF)
        nm[rows_at(t), :] = low
        gctx[fields_at(t)] = dot(low, wp[...], NT).astype(BF).reshape(per, TF, D)
        mlp_gain, mlp_bias = mlp_gain + row_sums(e * n), mlp_bias + row_sums(e)
        rim_totals(fields_at(t))
        send_rims(fields_at(t))
        place(f"E{t}")()

    d_up = remote(dst.at[0], hdst.at[1], back_s.at[4], back_r.at[5], up)
    d_dn = remote(dst.at[1], hdst.at[0], back_s.at[5], back_r.at[4], down)
    pl.when(has_up)(d_up.start)
    pl.when(has_down)(d_dn.start)
    pj = pn.chunks
    place("P")()
    put(pj, 0, D, dot(ctx[...], nm[...], TN))
    place("P1")()

    grad_joined = gpre

    def joined(g, j):
        return slice((3 * g + j) * WIDE, (3 * g + j + 1) * WIDE)

    def edge_rows(g, side, f):
        return pl.ds(pl.multiple_of(((g * 2 + side) * FD + f) * C, C), C)

    def back_group(g, hooks):
        def back_fields(i, carry):
            for when, do in hooks.items():
                pl.when(i == when)(do)
            units = [(i * fpi + j, r) for j in range(fpi) for r in range(R)]
            have = []
            for f, r in units:
                win = slice(r * C, (r + 3) * C)
                qd = widened(qb[span(f, r), k_lanes[g]])
                dod = widened(gctx[f, r * C : (r + 1) * C, k_lanes[g]])
                have.append((qd, dod, kv[f, win, k_lanes[g]], kv[f, win, v_lanes[g]], pt[f, g * R + r]))
            dps = [dot(v, dod, NT) for qd, dod, k, v, p in have]
            dss = []
            for (qd, dod, k, v, p), dp in zip(have, dps):
                wide = p.astype(F32)
                pd = wide * dp
                total = row_sums(pd)
                dss.append(((pd - wide * total) * SCALE).astype(BF))
            dqs = [diagonal(dot(ds, one[2], TN)).astype(BF) for ds, one in zip(dss, have)]
            dks, dvs = [], []
            for (f, r), ds, (qd, dod, k, v, p) in zip(units, dss, have):
                own = slice(C if r == 0 else 0, 2 * C if r == R - 1 else 3 * C)
                first = r + 1 if r == 0 else r
                dks.append((first, dot(ds[own], qd)))
                dvs.append((first, dot(p[own], dod)))
            for (f, r), o in zip(units, dqs):
                grad_joined[span(f, r), joined(g, 0)] = o
            for j in range(fpi):
                f = i * fpi + j
                for what, terms in enumerate((dks, dvs)):
                    for row in range(1, R + 1):
                        total = None
                        for first, term in terms[j * R : (j + 1) * R]:
                            if first <= row < first + term.shape[0] // C:
                                piece = term[(row - first) * C : (row - first + 1) * C]
                                total = piece if total is None else total + piece
                        if row in (1, R):
                            edge[edge_rows(g, 0 if row == 1 else 1, f), what * WIDE : (what + 1) * WIDE] = total
                        else:
                            grad_joined[span(f, row - 1), joined(g, what + 1)] = total.astype(BF)
            return carry

        lax.fori_loop(0, FD // fpi, back_fields, 0)
    def rim_part(h):
        return pl.ds(h * half, half)

    def back_edges(g, sent):
        for to_up, to_dn in sent:
            pl.when(has_up)(to_dn.wait_recv)
            pl.when(has_down)(to_up.wait_recv)

        def back_rims(h):
            units = [(h * half + j, side) for j in range(half) for side in range(2)]
            oks, rows = (has_up, has_down), (0, R - 1)
            have = []
            for f, side in units:
                qd = widened(hq[side, f * C : (f + 1) * C, k_lanes[g]])
                dod = widened(hg[side, f, :, k_lanes[g]])
                keys = slice((rows[side] + 1) * C, (rows[side] + 2) * C)
                have.append((qd, dod, kv[f, keys, k_lanes[g]], kv[f, keys, v_lanes[g]]))
            scores = [dot(k, qd, NT) for qd, dod, k, v in have]
            dps = [dot(v, dod, NT) for qd, dod, k, v in have]
            ps, dss = [], []
            for (f, side), s, dp in zip(units, scores, dps):
                s = (s + biasb[f]) * (SCALE * LOG2E) - hlse[side, pl.ds(f * 2 + g, 1), :]
                p = jnp.where(oks[side], jnp.exp2(s), 0.0)
                ds = p * (dp - hdst[side, pl.ds(f * 2 + g, 1), :]) * SCALE
                ps.append(p.astype(BF))
                dss.append(jnp.where(oks[side], ds, 0.0).astype(BF))
            dks = [dot(ds, one[0]) for ds, one in zip(dss, have)]
            dvs = [dot(p, one[1]) for p, one in zip(ps, have)]
            held = [edge[edge_rows(g, side, f), :] for f, side in units]
            for (f, side), dk, dv, own in zip(units, dks, dvs, held):
                dk = own[:, :WIDE] + jnp.where(oks[side], dk, 0.0)
                dv = own[:, WIDE:] + jnp.where(oks[side], dv, 0.0)
                grad_joined[span(f, rows[side]), joined(g, 1)] = dk.astype(BF)
                grad_joined[span(f, rows[side]), joined(g, 2)] = dv.astype(BF)

        for h in range(2):
            if g == 0:
                pl.when(has_up)(lambda: arrived(hg.at[0, rim_part(h)], rim_r.at[0, h]))
                pl.when(has_down)(lambda: arrived(hg.at[1, rim_part(h)], rim_r.at[1, h]))
            back_rims(h)
            place(f"X{2 * g + h + 1}")()
        put(pj + 1 + g, 0, D, dot(normed[...], grad_joined[:, 3 * g * WIDE : 3 * (g + 1) * WIDE], TN))
        place(f"C{g}")()

    back_group(0, {i: place(f"A{i}") for i in range(4)})
    back_group(1, {i: place(f"B{i}") for i in range(4)})
    for t in range(tiles):
        nm[rows_at(t), :] = (res[rows_at(t), :] + dot(act[rows_at(t), :], wo[...])).astype(BF)
        place(f"D{t}")()
    layer_copy = pltpu.make_async_copy(nm, out_layer, out_sem.at[0])
    layer_copy.start()

    place("X")()
    back_edges(0, ((l_up, l_dn), (d_up, d_dn)))
    back_edges(1, ())

    attn_gain, attn_bias = zero, zero

    def grad_of(t):
        e = None
        for g in range(2):
            for j in range(3):
                w = wq[:, j * D + g * WIDE : j * D + (g + 1) * WIDE]
                term = dot(grad_joined[rows_at(t), joined(g, j)], w, NT)
                e = term if e is None else e + term
        return e

    grad_in = grad_of(0)
    for t in range(tiles):
        e = grad_in
        if t + 1 < tiles:
            grad_in = grad_of(t + 1)
        n, rstd = normalize(pb[fields_at(t)].reshape(tile, D).astype(F32))
        gres[rows_at(t), :] += norm_pull(e, ga, n, rstd)
        attn_gain, attn_bias = attn_gain + row_sums(e * n), attn_bias + row_sums(e)
        place(f"F{t}")()

    patch_copy = pltpu.make_async_copy(gres, out_patch, out_sem.at[1])
    patch_copy.start()
    vec[...] = jnp.concatenate([attn_gain, attn_bias, mlp_gain, mlp_bias, zero, zero, zero, zero], axis=0)
    place("V0")()

    place("T")()
    while any(a <= b for a, b in zip(reached, last_step)):
        for k in sorted(range(vec_at + 1), key=lambda k: reached[k] - last_step[k], reverse=True):
            hook(codes[k])()

    for to_up, to_dn in halo_copies:
        pl.when(has_up)(to_up.wait_send)
        pl.when(has_down)(to_dn.wait_send)
    for h in range(2):
        pl.when(has_up)(lambda: arrived(hg.at[1, rim_part(h)], rim_s.at[0, h]))
        pl.when(has_down)(lambda: arrived(hg.at[0, rim_part(h)], rim_s.at[1, h]))
    for to_up, to_dn in ((l_up, l_dn), (d_up, d_dn)):
        pl.when(has_up)(to_up.wait_send)
        pl.when(has_down)(to_dn.wait_send)
    layer_copy.wait()
    patch_copy.wait()
    pltpu.make_async_copy(vec, out_vec, in_sem.at[0]).wait()
    for part in every:
        finish(part)


def widen(plan, *refs):
    pn = plan
    np_ = len(pn.sizes)
    ag, vec, layer, patch = refs[:np_], refs[np_], refs[np_ + 1], refs[np_ + 2]
    o_layer, o_patch, o_ag, o_ab, o_qkv, o_proj, o_mg, o_mb, o_hid, o_out = refs[np_ + 3 : np_ + 13]
    sc = list(refs[np_ + 13 :])
    low, wide = sc[:np_], sc[np_ : 2 * np_]
    kept_layer, kept_patch, in_sem, out_sem, pass_sem = sc[2 * np_ :]
    D = pn.width
    loads = [pltpu.make_async_copy(ag[p], low[p], in_sem.at[p]) for p in range(np_)]
    for c in loads:
        c.start()
    through = [
        (pltpu.make_async_copy(a, b, pass_sem.at[2 * i]), pltpu.make_async_copy(b, c, pass_sem.at[2 * i + 1]))
        for i, (a, b, c) in enumerate(((layer, kept_layer, o_layer), (patch, kept_patch, o_patch)))
    ]
    for arrive, _ in through:
        arrive.start()
    for i, o in enumerate((o_ag, o_ab, o_mg, o_mb)):
        o[...] = vec[i : i + 1, :].reshape(D)
    stores = []

    def store(src, dst):
        c = pltpu.make_async_copy(src, dst, out_sem.at[len(stores)])
        c.start()
        stores.append(c)

    def spread(p, start, rows, blocks, col):
        for j in range(blocks):
            wide[p][:, col + j * 128 : col + (j + 1) * 128] = low[p][
                start + j * rows : start + (j + 1) * rows, :
            ].astype(F32)

    for p in range(np_):
        loads[p].wait()
        if p == np_ - 1:
            for arrive, leave in through:
                arrive.wait()
                leave.start()
        if p < pn.chunks:
            spread(p, 0, CHUNK, D // 128, 0)
            store(wide[p].at[:, pl.ds(0, D)], o_out.at[pl.ds(p * CHUNK, CHUNK)])
            spread(p, CHUNK * (D // 128), D, CHUNK // 128, D)
            store(wide[p].at[:, pl.ds(D, CHUNK)], o_hid.at[:, pl.ds(p * CHUNK, CHUNK)])
        elif p == pn.chunks:
            spread(p, 0, D, D // 128, 0)
            store(wide[p], o_proj)
        else:
            g = p - pn.chunks - 1
            spread(p, 0, D, 3 * WIDE // 128, 0)
            for j in range(3):
                store(
                    wide[p].at[:, pl.ds(j * WIDE, WIDE)],
                    o_qkv.at[:, pl.ds(j * D + g * WIDE, WIDE)],
                )
    for c in stores + [leave for _, leave in through]:
        c.wait()


def per_device(mesh, patches, segment_ids, gain_attn, bias_attn, w_qkv, w_proj, gain_mlp, bias_mlp, w_hidden, w_output, cotangent):
    fields, rows, cols, width = patches.shape
    ff = w_hidden.shape[1]
    pn = Plan(mesh, fields, rows, cols, width, ff)
    np_ = len(pn.sizes)
    T, TF, D, C, R, FD = pn.tokens, pn.tf, width, cols, rows, fields
    L, Z = pn.lats, pn.zs
    anywhere = pl.BlockSpec(memory_space=pl.ANY)
    vmem = pl.BlockSpec(memory_space=pltpu.VMEM)
    V = pltpu.VMEM
    dma = pltpu.SemaphoreType.DMA
    scratch = [
        V((D, 3 * D), BF), V((D, D), BF), V((D, ff), BF), V((ff, D), BF),
        V((FD, TF, D), BF), V((T, D), BF), V(segment_ids.shape, jnp.int32), V((2, FD, C, D), BF),
        V((T, D), BF), V((T, D), BF), V((FD, TF + 2 * C, 2 * D), BF), V((FD, 2 * R, 3 * C, WIDE), BF),
        V((T, D), BF), V((T, D), F32), V((T, D), BF), V((T, D), F32),
        V((T, ff), BF), V((T, ff), BF), V((FD, TF, D), BF),
        V((max(4 * FD * C, T), 2 * WIDE), F32),
        V((2, FD * C, D), BF), V((2, FD, C, D), BF),
        V((2, 2 * FD, WIDE), F32), V((2, 2 * FD, WIDE), F32), V((2, 2 * FD, WIDE), F32), V((2, 2 * FD, WIDE), F32),
        V((WIDE, WIDE), BF), V((FD, C, WIDE), F32),
        V((8, D), F32), V((Z, 8, D), F32), V((L, 8, D), F32), V((2, 8, D), F32),
    ]
    scratch += [V((n, 128), BF) for n in pn.sizes]
    scratch += [V((n, 128), BF) for n in pn.landing]
    scratch += [V((n, 128), BF) for n in pn.sizes]
    scratch += [
        dma((7,)), dma((2 + pn.n_subs,)), dma((2, 2)), dma((2, 2)), dma((2, 2)), dma((2, 2)), dma((8,)), dma((8,)),
        dma((pn.n_subs, 8)), dma((pn.n_subs, 8)), dma((3,)), dma((3,)),
    ]
    shape = jax.ShapeDtypeStruct
    outs = pl.pallas_call(
        functools.partial(body, pn),
        out_shape=[shape((T, D), BF), shape((T, D), F32), shape((8, D), F32)]
        + [shape((n, 128), BF) for n in pn.sizes],
        in_specs=[anywhere, anywhere, vmem, vmem, anywhere, anywhere, vmem, vmem, anywhere, anywhere, anywhere],
        out_specs=[anywhere] * (3 + np_),
        scratch_shapes=scratch,
        compiler_params=pltpu.CompilerParams(
            collective_id=0, has_side_effects=True, vmem_limit_bytes=62 * 2**20
        ),
        name="block",
    )(
        patches.reshape(FD, TF, D), segment_ids, gain_attn, bias_attn, w_qkv, w_proj, gain_mlp, bias_mlp,
        w_hidden, w_output, cotangent.reshape(T, D),
    )
    layer, patch, vec = outs[:3]
    ags = outs[3:]
    wides = [(D, D + CHUNK)] * pn.chunks + [(D, D)] + [(D, 3 * WIDE)] * 2
    final = pl.pallas_call(
        functools.partial(widen, pn),
        out_shape=[
            shape((T, D), BF), shape((T, D), F32), shape((D,), F32), shape((D,), F32), shape((D, 3 * D), F32),
            shape((D, D), F32), shape((D,), F32), shape((D,), F32), shape((D, ff), F32), shape((ff, D), F32),
        ],
        in_specs=[anywhere] * np_ + [vmem, anywhere, anywhere],
        out_specs=[anywhere, anywhere, vmem, vmem, anywhere, anywhere, vmem, vmem, anywhere, anywhere],
        scratch_shapes=[V((n, 128), BF) for n in pn.sizes]
        + [V(s, F32) for s in wides]
        + [V((T, D), BF), V((T, D), F32), dma((np_,)), dma((2 * pn.chunks + 7,)), dma((4,))],
        compiler_params=pltpu.CompilerParams(vmem_limit_bytes=62 * 2**20),
        name="widen",
    )(*ags, vec, layer, patch)
    block = (FD, R, C, D)
    return (final[0].reshape(block), final[1].reshape(block)) + tuple(final[2:])


def solution(mesh):
    band = P("fld", "lat", None, None)
    return jax.shard_map(
        functools.partial(per_device, mesh),
        mesh=mesh,
        in_specs=(band, P("fld", None, None)) + (P(),) * 8 + (band,),
        out_specs=(band, band) + (P(),) * 8,
        check_vma=False,
    )
```

profile of v0, /device:TPU:1, one launch (start us, length us, event | category | flops | bytes accessed | tf_op | source)
XLA Modules:
  0.0 124.1 jit_solution(15457171729499931230)
XLA Ops:
  0.6 112.7 %block.1 = (bf16[1024,512]{1,0:T(8,128)(2,1)}, f32[1024,512]{1,0:T(8,128)}, f32[8,512]{1,0:T(8,128)}, bf16[4096,128]{1,0:T(8,128)(2,1)}, bf16[4096,128]{1,0:T(8,...) custom-call(bf16[8,128,512]{2,1,0:T(8,128)(2,1)} %bitcast.4, ...), custom_call_target="tpu_custom_call" | custom-call | tf_op jit(solution)/shard_map/block/pallas_call | solution.py:823
  113.4 10.5 %widen.1 = (bf16[1024,512]{1,0:T(8,128)(2,1)}, f32[1024,512]{1,0:T(8,128)}, f32[512]{0:T(512)}, f32[512]{0:T(512)}, f32[512,1536]{1,0:T(8,128)}, /*index=5*/f32[...) custom-call(bf16[4096,128]{1,0:T(8,128)(2,1)} %get-tuple-element.30.refs_0_, ...), custom_call_target="tpu_custom_call" | custom-call | tf_op jit(solution)/shard_map/widen/pallas_call | solution.py:841
where the time goes:
time: 126 us; the launch traced here: 124 us
  Pallas kernels  123 us (98%)
    pallas_call x1, Pallas kernels, per_device(): pl.pallas_call(functools.partial(body, pn), out_shape=[shape((T, D), BF),...  113 us
    pallas_call x1, Pallas kernels, per_device(): pl.pallas_call(functools.partial(widen, pn), out_shape=[shape((T, D), BF)...  10.5 us

commit v1 on v0

--- a/solution.py
+++ b/solution.py
@@ -51,7 +51,7 @@
     "F2": (1, 7, 12),
     "F3": (9, 2),
     "V0": (14,),
-    "T": (6, 1, 8, 3, 5, 10, 14, 7, 9, 4, 8, 12, 10, 14, 2, 6, 5, 7, 9, 3, 12, 14, 2, 8, 3, 4, 10, 5, 6, 4, 12, 5, 8, 7, 6, 9, 8, 7, 9, 10, 10, 12, 12),
+    "T": (6, 1, 8, 3, 5, 10, 7, 9, 4, 8, 14, 12, 10, 2, 6, 5, 7, 2, 9, 3, 12, 8, 3, 4, 10, 14, 5, 12, 14, 4, 6, 7, 8, 9, 5, 10, 6, 7, 8, 9, 10, 12, 12),
 }
 BF = jnp.bfloat16
 F32 = jnp.float32

time: 126 us -> 125 us (level)
  no operation moved by 1% of the time
where the time goes in v1:
time: 125 us; the launch traced here: 124 us
  Pallas kernels  123 us (98%)
    pallas_call x1, Pallas kernels, per_device(): pl.pallas_call(functools.partial(body, pn), out_shape=[shape((T, D), BF),...  113 us
    pallas_call x1, Pallas kernels, per_device(): pl.pallas_call(functools.partial(widen, pn), out_shape=[shape((T, D), BF)...  10.5 us

profile of v1, /device:TPU:1, one launch (start us, length us, event | category | flops | bytes accessed | tf_op | source)
XLA Modules:
  0.0 124.1 jit_solution(9190938890855137869)
XLA Ops:
  0.6 112.7 %block.1 = (bf16[1024,512]{1,0:T(8,128)(2,1)}, f32[1024,512]{1,0:T(8,128)}, f32[8,512]{1,0:T(8,128)}, bf16[4096,128]{1,0:T(8,128)(2,1)}, bf16[4096,128]{1,0:T(8,...) custom-call(bf16[8,128,512]{2,1,0:T(8,128)(2,1)} %bitcast.4, ...), custom_call_target="tpu_custom_call" | custom-call | tf_op jit(solution)/shard_map/block/pallas_call | solution.py:823
  113.4 10.5 %widen.1 = (bf16[1024,512]{1,0:T(8,128)(2,1)}, f32[1024,512]{1,0:T(8,128)}, f32[512]{0:T(512)}, f32[512]{0:T(512)}, f32[512,1536]{1,0:T(8,128)}, /*index=5*/f32[...) custom-call(bf16[4096,128]{1,0:T(8,128)(2,1)} %get-tuple-element.30.refs_0_, ...), custom_call_target="tpu_custom_call" | custom-call | tf_op jit(solution)/shard_map/widen/pallas_call | solution.py:841

commit v2 on v1

--- a/solution.py
+++ b/solution.py
@@ -19,7 +19,7 @@
 CHUNK = 512
 BLOCK = 256
 FIELDS_AT_ONCE = 2
-DIRECT = (5, 6)
+DIRECT = ()
 Z_FIRST = ()
 SCHEDULE = {
     "J2": (0, 1),
@@ -43,15 +43,15 @@
     "X": (2,),
     "X1": (1, 5, 4, 0, 8),
     "X2": (3, 7),
-    "C0": (9, 6, 10),
+    "C0": (9, 6, 10, 11),
     "X3": (8, 1, 2),
-    "X4": (10, 5),
-    "C1": (0, 4, 12),
+    "X4": (10, 11, 5),
+    "C1": (0, 4, 12, 13),
     "F1": (3, 0),
-    "F2": (1, 7, 12),
-    "F3": (9, 2),
+    "F2": (12, 1, 7, 13),
+    "F3": (10, 9, 2),
     "V0": (14,),
-    "T": (6, 1, 8, 3, 5, 10, 7, 9, 4, 8, 14, 12, 10, 2, 6, 5, 7, 2, 9, 3, 12, 8, 3, 4, 10, 14, 5, 12, 14, 4, 6, 7, 8, 9, 5, 10, 6, 7, 8, 9, 10, 12, 12),
+    "T": (6, 1, 8, 3, 11, 5, 12, 13, 4, 7, 9, 8, 10, 2, 11, 6, 14, 13, 2, 5, 12, 3, 10, 8, 11, 4, 13, 3, 7, 12, 9, 4, 5, 10, 13, 14, 6, 12, 11, 5, 13, 14, 12, 8, 7, 9, 6, 10, 11, 13, 13, 12, 8, 7, 9, 11, 12, 10, 11, 10),
 }
 BF = jnp.bfloat16
 F32 = jnp.float32

time: 125 us -> 125 us (level)
  no operation moved by 1% of the time
where the time goes in v2:
time: 125 us; the launch traced here: 124 us
  Pallas kernels  124 us (99%)
    pallas_call x1, Pallas kernels, per_device(): pl.pallas_call(functools.partial(body, pn), out_shape=[shape((T, D), BF),...  113 us
    pallas_call x1, Pallas kernels, per_device(): pl.pallas_call(functools.partial(widen, pn), out_shape=[shape((T, D), BF)...  10.5 us

profile of v2, /device:TPU:1, one launch (start us, length us, event | category | flops | bytes accessed | tf_op | source)
XLA Modules:
  0.0 124.4 jit_solution(10286482263585295885)
XLA Ops:
  0.6 113.1 %block.1 = (bf16[1024,512]{1,0:T(8,128)(2,1)}, f32[1024,512]{1,0:T(8,128)}, f32[8,512]{1,0:T(8,128)}, bf16[4096,128]{1,0:T(8,128)(2,1)}, bf16[4096,128]{1,0:T(8,...) custom-call(bf16[8,128,512]{2,1,0:T(8,128)(2,1)} %bitcast.4, ...), custom_call_target="tpu_custom_call" | custom-call | tf_op jit(solution)/shard_map/block/pallas_call | solution.py:823
  113.7 10.5 %widen.1 = (bf16[1024,512]{1,0:T(8,128)(2,1)}, f32[1024,512]{1,0:T(8,128)}, f32[512]{0:T(512)}, f32[512]{0:T(512)}, f32[512,1536]{1,0:T(8,128)}, /*index=5*/f32[...) custom-call(bf16[4096,128]{1,0:T(8,128)(2,1)} %get-tuple-element.30.refs_0_, ...), custom_call_target="tpu_custom_call" | custom-call | tf_op jit(solution)/shard_map/widen/pallas_call | solution.py:841
